TPU v7x, 32 devices: a whole 2x2x4 slice. The times are simulated.
32 devices in a mesh: groups: 2 (over x), seq: 16 (over z, y, core).
Axes of the slice: x: 2, y: 2, z: 4, core: 2. Of those that a mesh axis runs over, the one named last changes fastest.
Arguments:
- queries: bfloat16 [10240, 4096], P(('groups', 'seq')), parts along dimension 0, may hold values from -6 to 6
- keys: bfloat16 [10240, 4096], P(('groups', 'seq')), parts along dimension 0, may hold values from -6 to 6
- values: bfloat16 [10240, 4096], P(('groups', 'seq')), parts along dimension 0, may hold values from -6 to 6
- doc_starts: int32 [32, 2], P(('groups', 'seq')), parts along dimension 0, may hold values from 0 to 320, as said below
- previous_window_states: bfloat16 [64, 32, 128, 128], P(('groups', 'seq')), parts along dimension 0, may hold values from -80 to 80
- out_gain: float32 [4096], replicated, may hold values from 0.1 to 1.9
Outputs:
- attended: bfloat16 [10240, 4096], P(('groups', 'seq')), parts along dimension 0
There are 2 independent parts, one for each index of `groups`. A program takes and returns all parts, laid end to end along the dimension named above; an argument that names none is the same for every part. Nothing has to cross between parts.
Inputs may be any that keep to these rules, and one draw needn't show every extreme that they name: `doc_starts`: each row holds the offsets of document starts in that block of 320 tokens, ascending, with 320 in unused entries; row 0 begins with 0; every document has at most 3840 tokens, and one has exactly that many; some row holds 2 starts.
All inputs are finite; a program needn't handle non-finite values.
Results may differ from a plain program's by a relative error of at most 0.0049.
Values sent between devices are 32-bit elements; how exact they have to be, the bound alone decides.
A program may use at most 128 MiB of HBM per device.

v0:
```python
import jax
import jax.numpy as jnp
from jax import lax
from jax.sharding import PartitionSpec as P

HEAD_COUNT = 32
KEY_DIM = 128
VALUE_DIM = 128
DOCUMENT_BLOCKS = 12


EPSILON = 1e-06


def from_behind(value, axis, steps):
    count = lax.axis_size(axis)
    first, last = (max(0, -steps), min(count, count - steps))
    return lax.ppermute(value, axis, [(source, source + steps) for source in range(first, last)])


def features(raw):
    return jax.nn.silu(raw.astype(jnp.float32)).astype(jnp.bfloat16)


def segment_numbers(starts, rows_here):
    position = jnp.arange(rows_here, dtype=jnp.int32)
    segment = jnp.sum((starts[None, :] <= position[:, None]).astype(jnp.int32), axis=1)
    last_segment = jnp.sum((starts < rows_here).astype(jnp.int32))
    return (position, segment, last_segment)


def block_terms(query_feat, key_feat, value_block, starts, carried_block):
    rows_here = query_feat.shape[0]
    position, segment, last_segment = segment_numbers(starts, rows_here)
    allowed = (position[:, None] >= position[None, :]) & (segment[:, None] == segment[None, :])
    scores = jnp.einsum("thd,shd->hts", query_feat, key_feat, preferred_element_type=jnp.float32)
    scores = jnp.where(allowed[None], scores, 0.0).astype(jnp.bfloat16)
    within = jnp.einsum("hts,she->the", scores, value_block, preferred_element_type=jnp.float32)
    resumed_terms = jnp.einsum(
        "thd,mhde->mthe", query_feat, carried_block, preferred_element_type=jnp.float32
    )
    member_ids = jnp.arange(carried_block.shape[0], dtype=jnp.int32)
    for member in range(carried_block.shape[0]):
        within = within + jnp.where(
            (segment == member + 1)[:, None, None], resumed_terms[member], 0.0
        )
    picked = (member_ids + 1 == last_segment).astype(jnp.float32)
    initial = jnp.sum(picked[:, None, None, None] * carried_block.astype(jnp.float32), axis=0)
    tail_keys = jnp.where(
        (segment == last_segment)[:, None, None], key_feat, jnp.zeros_like(key_feat)
    )
    summary = (
        jnp.einsum("thd,the->hde", tail_keys, value_block, preferred_element_type=jnp.float32)
        + initial
    )
    started = jnp.reshape((last_segment > 0).astype(jnp.float32), (1,))
    return (within, segment, started, summary)


def combine(earlier, later):
    return (
        jnp.maximum(earlier[0], later[0]),
        jnp.where(later[0][0] > 0, later[1], earlier[1] + later[1]),
    )


def on_device(queries, keys, values, doc_starts, previous_window_states, out_gain):
    rows_here = queries.shape[0]
    query_feat = features(queries).reshape(rows_here, HEAD_COUNT, KEY_DIM)
    key_feat = features(keys).reshape(rows_here, HEAD_COUNT, KEY_DIM)
    value_block = values.reshape(rows_here, HEAD_COUNT, VALUE_DIM)
    within, segment, started, summary = block_terms(
        query_feat, key_feat, value_block, doc_starts[0], previous_window_states
    )
    distances = [1]
    covered = 1
    while covered < DOCUMENT_BLOCKS:
        distances.append(covered)
        covered = covered * 2
    running = (started, summary)
    for number, distance in enumerate(distances):
        moved = from_behind((running[0], running[1]), "seq", distance)
        running = moved if number == 0 else combine(moved, running)
    incoming = running[1]
    query_wide = query_feat.astype(jnp.float32)
    cross = jnp.einsum("thd,hde->the", query_wide, incoming, precision=lax.Precision.HIGHEST)
    total = within + jnp.where((segment == 0)[:, None, None], cross, 0.0)
    flat = total.reshape(rows_here, -1)
    mean_square = jnp.mean(flat * flat, axis=1, keepdims=True)
    return (flat * lax.rsqrt(mean_square + EPSILON) * out_gain).astype(jnp.bfloat16)


def solution(mesh):
    placed = (
        P(("groups", "seq"), None),
        P(("groups", "seq"), None),
        P(("groups", "seq"), None),
        P(("groups", "seq"), None),
        P(("groups", "seq"), None, None, None),
        P(),
    )
    return jax.shard_map(
        on_device, mesh=mesh, in_specs=placed, out_specs=P(("groups", "seq"), None), check_vma=False
    )
```

profile of v0, /device:TPU:27, one launch (start us, length us, event | category | flops | bytes accessed | tf_op | source)
XLA Modules:
  0.0 274.5 jit_solution(15106806804335131467)
XLA Ops:
  0.0 0.0 copy-start
  0.0 0.0 copy-start.3
  0.0 1.4 fusion.46
  1.4 0.8 compare_convert_fusion.1
  2.2 0.7 fusion.45
  3.0 0.7 broadcast_compare_fusion
  3.6 2.4 multiply_reduce_fusion.1
  6.0 0.0 copy-done
  6.0 0.0 copy-done.3
  6.0 2.3 fusion.39
  8.3 3.7 %collective-permute-start.4 = (f32[32,128,128]{2,1,0:T(8,128)S(1)}, f32[32,128,128]{2,1,0:T(8,128)}, u32[]{:S(2)}, u32[]{:S(2)}) collective-permute-start(f32[32,128,128]{2,1,0:T(8,128)S(1)} %fusion.39), channel_id=1, source_target_pairs={{0,1},{1,2},{2,3},{3,4},{4,5},{5,6},{6,7},{7,8},{8,9},{9,10},{10,1... | collective-permute-start | bytes 6291464 | tf_op jit(solution)/shard_map/ppermute | solution.py:18
  12.1 23.0 %collective-permute-done.4 = f32[32,128,128]{2,1,0:T(8,128)} collective-permute-done((f32[32,128,128]{2,1,0:T(8,128)S(1)}, f32[32,128,128]{2,1,0:T(8,128)}, u32[]{:S(2)}, u32[]{:S(2)}) %collective-permute-start.4) | collective-permute-done | bytes 2097184 | tf_op jit(solution)/shard_map/ppermute | solution.py:18
  35.0 4.5 %collective-permute-start.5 = (f32[32,128,128]{2,1,0:T(8,128)}, f32[32,128,128]{2,1,0:T(8,128)}, u32[]{:S(2)}, u32[]{:S(2)}) collective-permute-start(f32[32,128,128]{2,1,0:T(8,128)} %collective-permute-done.4), channel_id=1, source_target_pairs={{0,1},{1,2},{2,3},{3,4},{4,5},{5,6},{6,7},{7,8},{8,9},{9,10},{10,1... | collective-permute-start | bytes 6291464 | tf_op jit(solution)/shard_map/ppermute | solution.py:18
  40.1 22.6 %collective-permute-start = (f32[1]{0:T(128)}, f32[1]{0:T(128)}, u32[]{:S(2)}, u32[]{:S(2)}) collective-permute-start(f32[1]{0:T(128)} %bitcast.6), channel_id=1, source_target_pairs={{0,1},{1,2},{2,3},{3,4},{4,5},{5,6},{6,7},{7,8},{8,9},{9,10},{10,1... | collective-permute-start | bytes 20 | tf_op jit(solution)/shard_map/ppermute | solution.py:18
  62.8 0.0 collective-permute-done
  63.5 0.0 collective-permute-done.5
  63.5 2.5 add_select_fusion.3
  66.0 1.9 collective-permute-start.6
  67.9 3.8 %collective-permute-start.1 = (f32[1]{0:T(128)}, f32[1]{0:T(128)}, u32[]{:S(2)}, u32[]{:S(2)}) collective-permute-start(f32[1]{0:T(128)} %collective-permute-done), channel_id=1, source_target_pairs={{0,1},{1,2},{2,3},{3,4},{4,5},{5,6},{6,7},{7,8},{8,9},{9,10},{10,1... | collective-permute-start | bytes 20 | tf_op jit(solution)/shard_map/ppermute | solution.py:18
  71.7 38.3 %collective-permute-done.1 = f32[1]{0:T(128)} collective-permute-done((f32[1]{0:T(128)}, f32[1]{0:T(128)}, u32[]{:S(2)}, u32[]{:S(2)}) %collective-permute-start.1) | collective-permute-done | bytes 36 | tf_op jit(solution)/shard_map/ppermute | solution.py:18
  111.3 1.5 collective-permute-done.6
  112.8 0.0 copy-start.1
  112.8 0.0 copy-start.4
  112.8 0.3 add_select_fusion.2
  113.1 1.6 collective-permute-start.7
  114.6 0.0 copy-done.1
  114.6 0.5 copy-done.4
  115.1 5.5 %convolution_bitcast_fusion = f32[2,320,32,128]{3,1,2,0:T(8,128)} fusion(bf16[2,32,128,128]{3,2,1,0:T(8,128)(2,1)S(1)} %copy-done.1, bf16[320,4096]{1,0:T(8,128)(2,1)S(1)} %copy-done.4), kind=kOutput, calls=%fused_computation.25 | convolution fusion | flops 678952960 | bytes 15204352 | tf_op jit(solution)/shard_map/thd,mhde->mthe/dot_general | solution.py:39
  120.6 2.6 collective-permute-start.2
  123.3 39.3 %collective-permute-done.2 = f32[1]{0:T(128)} collective-permute-done((f32[1]{0:T(128)}, f32[1]{0:T(128)}, u32[]{:S(2)}, u32[]{:S(2)}) %collective-permute-start.2) | collective-permute-done | bytes 36 | tf_op jit(solution)/shard_map/ppermute | solution.py:18
  163.1 0.0 collective-permute-done.7
  163.1 1.7 add_select_fusion.1
  164.9 1.3 collective-permute-start.8
  166.1 0.1 fusion.44
  166.3 8.6 %fusion.19 = f32[32,320,128]{2,1,0:T(8,128)} fusion(pred[320,320]{1,0:T(8,128)(4,1)S(1)} %fusion.44, bf16[320,4096]{1,0:T(8,128)(2,1)S(1)} %copy-done, bf16[320,4096]{1,0:T(8,128)(2,1)} %param.7, bf16[320,4096]{1,0:T(8,128)(2,1)} %param.6), kind=kOutput, calls=%fused_computation.34 | convolution fusion | flops 1700003840 | bytes 13209600 | tf_op jit(solution)/shard_map/hts,she->the/dot_general | solution.py:38
  174.9 1.5 collective-permute-start.3
  176.3 2.8 %collective-permute-done.3 = f32[1]{0:T(128)} collective-permute-done((f32[1]{0:T(128)}, f32[1]{0:T(128)}, u32[]{:S(2)}, u32[]{:S(2)}) %collective-permute-start.3) | collective-permute-done | bytes 36 | tf_op jit(solution)/shard_map/ppermute | solution.py:18
  179.7 79.8 %collective-permute-done.8 = f32[32,128,128]{2,1,0:T(8,128)} collective-permute-done((f32[32,128,128]{2,1,0:T(8,128)}, f32[32,128,128]{2,1,0:T(8,128)}, u32[]{:S(2)}, u32[]{:S(2)}) %collective-permute-start.8) | collective-permute-done | bytes 2097184 | tf_op jit(solution)/shard_map/ppermute | solution.py:18
  259.5 0.0 copy-start.2
  259.5 12.9 %multiply_reduce_fusion = (f32[320]{0:T(512)S(1)}, f32[320,32,128]{2,0,1:T(8,128)S(1)}) fusion(f32[32,128,128]{2,1,0:T(8,128)} %add_select_fusion.1, f32[32,128,128]{2,1,0:T(8,128)} %collective-permute-done.8, pred[]{:T(512)} %bitcast.7, pred[320]{0:T(512)(128)(4,1)S(1)} %get-tuple-element.6, f32[2,320,32,128]{3,1,2,0:T(8,128)} %convolution_bitcast_fusion, ...), kind=kOutput, calls=%fused_computation.23 | convolution fusion | flops 2032664320 | bytes 27789504 | tf_op jit(solution)/shard_map/thd,hde->the/dot_general | solution.py:86
  272.4 0.0 copy-done.2
  272.4 2.1 fusion.9
  (1 shorter events, 0.0 us)
Async XLA Ops:
  0.0 6.0 %copy-start = (bf16[320,4096]{1,0:T(8,128)(2,1)S(1)}, bf16[320,4096]{1,0:T(8,128)(2,1)}, u32[]{:S(2)}) copy-start(bf16[320,4096]{1,0:T(8,128)(2,1)} %param.8) | copy-start | bytes 7864324
  0.0 6.0 %copy-start.3 = (bf16[320,4096]{1,0:T(8,128)(2,1)S(1)}, bf16[320,4096]{1,0:T(8,128)(2,1)}, u32[]{:S(2)}) copy-start(bf16[320,4096]{1,0:T(8,128)(2,1)} %param.7) | copy-start | bytes 7864324
  8.3 26.7 %collective-permute-start.4 = (f32[32,128,128]{2,1,0:T(8,128)S(1)}, f32[32,128,128]{2,1,0:T(8,128)}, u32[]{:S(2)}, u32[]{:S(2)}) collective-permute-start(f32[32,128,128]{2,1,0:T(8,128)S(1)} %fusion.39), channel_id=1, source_target_pairs={{0,1},{1,2},{2,3},{3,4},{4,5},{5,6},{6,7},{7,8},{8,9},{9,10},{10,1... | collective-permute-start | bytes 6291464 | tf_op jit(solution)/shard_map/ppermute | solution.py:18
  35.0 28.5 %collective-permute-start.5 = (f32[32,128,128]{2,1,0:T(8,128)}, f32[32,128,128]{2,1,0:T(8,128)}, u32[]{:S(2)}, u32[]{:S(2)}) collective-permute-start(f32[32,128,128]{2,1,0:T(8,128)} %collective-permute-done.4), channel_id=1, source_target_pairs={{0,1},{1,2},{2,3},{3,4},{4,5},{5,6},{6,7},{7,8},{8,9},{9,10},{10,1... | collective-permute-start | bytes 6291464 | tf_op jit(solution)/shard_map/ppermute | solution.py:18
  40.1 22.6 %collective-permute-start = (f32[1]{0:T(128)}, f32[1]{0:T(128)}, u32[]{:S(2)}, u32[]{:S(2)}) collective-permute-start(f32[1]{0:T(128)} %bitcast.6), channel_id=1, source_target_pairs={{0,1},{1,2},{2,3},{3,4},{4,5},{5,6},{6,7},{7,8},{8,9},{9,10},{10,1... | collective-permute-start | bytes 20 | tf_op jit(solution)/shard_map/ppermute | solution.py:18
  66.0 46.8 %collective-permute-start.6 = (f32[32,128,128]{2,1,0:T(8,128)S(1)}, f32[32,128,128]{2,1,0:T(8,128)S(1)}, u32[]{:S(2)}, u32[]{:S(2)}) collective-permute-start(f32[32,128,128]{2,1,0:T(8,128)S(1)} %add_select_fusion.3), channel_id=1, source_target_pairs={{0,2},{1,3},{2,4},{3,5},{4,6},{5,7},{6,8},{7,9},{8,10},{9,11},{10,... | collective-permute-start | bytes 6291464 | tf_op jit(solution)/shard_map/ppermute | solution.py:18
  67.9 42.1 %collective-permute-start.1 = (f32[1]{0:T(128)}, f32[1]{0:T(128)}, u32[]{:S(2)}, u32[]{:S(2)}) collective-permute-start(f32[1]{0:T(128)} %collective-permute-done), channel_id=1, source_target_pairs={{0,1},{1,2},{2,3},{3,4},{4,5},{5,6},{6,7},{7,8},{8,9},{9,10},{10,1... | collective-permute-start | bytes 20 | tf_op jit(solution)/shard_map/ppermute | solution.py:18
  112.8 1.9 copy-start.1
  112.8 2.4 copy-start.4
  113.1 50.1 %collective-permute-start.7 = (f32[32,128,128]{2,1,0:T(8,128)S(1)}, f32[32,128,128]{2,1,0:T(8,128)S(1)}, u32[]{:S(2)}, u32[]{:S(2)}) collective-permute-start(f32[32,128,128]{2,1,0:T(8,128)S(1)} %add_select_fusion.2), channel_id=1, source_target_pairs={{0,4},{1,5},{2,6},{3,7},{4,8},{5,9},{6,10},{7,11},{8,12},{9,13},{1... | collective-permute-start | bytes 6291464 | tf_op jit(solution)/shard_map/ppermute | solution.py:18
  120.6 41.9 %collective-permute-start.2 = (f32[1]{0:T(128)}, f32[1]{0:T(128)}, u32[]{:S(2)}, u32[]{:S(2)}) collective-permute-start(f32[1]{0:T(128)} %max.9), channel_id=1, source_target_pairs={{0,2},{1,3},{2,4},{3,5},{4,6},{5,7},{6,8},{7,9},{8,10},{9,11},{10,... | collective-permute-start | bytes 20 | tf_op jit(solution)/shard_map/ppermute | solution.py:18
  164.9 94.6 %collective-permute-start.8 = (f32[32,128,128]{2,1,0:T(8,128)}, f32[32,128,128]{2,1,0:T(8,128)}, u32[]{:S(2)}, u32[]{:S(2)}) collective-permute-start(f32[32,128,128]{2,1,0:T(8,128)} %add_select_fusion.1), channel_id=1, source_target_pairs={{0,8},{1,9},{2,10},{3,11},{4,12},{5,13},{6,14},{7,15},{16,24},{17,... | collective-permute-start | bytes 6291464 | tf_op jit(solution)/shard_map/ppermute | solution.py:18
  174.9 4.2 %collective-permute-start.3 = (f32[1]{0:T(128)}, f32[1]{0:T(128)}, u32[]{:S(2)}, u32[]{:S(2)}) collective-permute-start(f32[1]{0:T(128)} %max.10), channel_id=1, source_target_pairs={{0,4},{1,5},{2,6},{3,7},{4,8},{5,9},{6,10},{7,11},{8,12},{9,13},{1... | collective-permute-start | bytes 20 | tf_op jit(solution)/shard_map/ppermute | solution.py:18
  259.5 12.9 %copy-start.2 = (f32[4096]{0:T(1024)S(1)}, f32[4096]{0:T(1024)}, u32[]{:S(2)}) copy-start(f32[4096]{0:T(1024)} %param.11) | copy-start | bytes 49156
where the time goes:
time: 276 us; the launch traced here: 275 us
  waiting for transfers between devices  185 us (67%)
  starting transfers between devices  43.4 us (16%)
  matrix products  29.3 us (11%)
  other arithmetic  12.8 us (5%)
  between operations  4.01 us (1%)
    ppermute x9, waiting for transfers between devices, from_behind(): lax.ppermute(value, axis, [(source, source + steps) for source in range(f...  185 us
    ppermute x9, starting transfers between devices, from_behind(): lax.ppermute(value, axis, [(source, source + steps) for source in range(f...  43.4 us
    dot_general x1, matrix products, on_device(): jnp.einsum('thd,hde->the', query_wide, incoming, precision=lax.Precision....  12.9 us
    dot_general x1, matrix products, block_terms(): jnp.einsum('hts,she->the', scores, value_block, preferred_element_type=jn...  8.58 us
  transfers between devices with their start and end apart: 9, of which 6 were waited for; matrix products, arithmetic and copies ran while one was open for 5% of the time, Pallas kernels for 0%

commit v1 on v0

v1 whole, which is shorter than its diff:
```python
import functools

import jax
import jax.numpy as jnp
from jax import lax
from jax.experimental import pallas as pl
from jax.experimental.pallas import tpu as pltpu
from jax.sharding import PartitionSpec as P

HEADS = 32
DIM = 128
PART = HEADS // 4
EPSILON = 1e-06
LAG = 9
ROWS_OUT = 32
MESH = pl.DeviceIdType.MESH


def silu(x):
    half = x.astype(jnp.float32) * 0.5
    return (half + half * jnp.tanh(half)).astype(jnp.bfloat16)


def kernel(
    starts, q_hbm, k_hbm, v_hbm, c_hbm, gain, out_hbm,
    q, k, v, c, o, obuf, acc, allowed, seg_masks, flags, coefs,
    state, near_a, near_b, chip_out, chip_own, chip_in, row, z_in, z_out, back_out, back_in,
    final_a, final_b, incoming,
    in_sem, out_sem, flag_send, flag_recv, send_sem, recv_sem,
):
    rows = q.shape[0]
    count = lax.axis_size("seq")
    me = lax.axis_index("seq")
    z = me // 4
    depth = count // 4
    y = (me // 2) % 2
    core = me % 2
    partner = me + 1 - 2 * core
    across = me + 2 - 4 * y
    following = lax.rem(me + 4, count)
    mine = y * 2 + core
    part_near = y * 2 + (1 - core)
    part_far = (1 - y) * 2 + core
    part_diag = (1 - y) * 2 + (1 - core)

    def load(slot, source, target, part):
        columns = pl.ds(pl.multiple_of(part * (PART * DIM), PART * DIM), PART * DIM)
        return pltpu.make_async_copy(source.at[:, columns], target.at[:, columns], in_sem.at[slot])

    def load_states(slot, part):
        heads = pl.ds(part * PART, PART)
        return pltpu.make_async_copy(c_hbm.at[:, heads], c.at[:, heads], in_sem.at[slot])

    order_kv = (part_diag, part_far, part_near, mine)
    order_q = (mine, part_near, part_far, part_diag)
    k_loads = [load(i, k_hbm, k, p) for i, p in enumerate(order_kv)]
    v_loads = [load(4 + i, v_hbm, v, p) for i, p in enumerate(order_kv)]
    c_loads = [load_states(8 + i, p) for i, p in enumerate(order_kv)]
    q_loads = [load(12 + i, q_hbm, q, p) for i, p in enumerate(order_q)]
    for i in range(4):
        k_loads[i].start()
        v_loads[i].start()
        c_loads[i].start()
    for i in range(4):
        q_loads[i].start()

    barrier = pltpu.get_barrier_semaphore()
    for other in (partner, across):
        pl.semaphore_signal(barrier, inc=1, device_id={"seq": other}, device_id_type=MESH)

    @pl.when(z > 0)
    def _():
        pl.semaphore_signal(barrier, inc=1, device_id={"seq": me - 4}, device_id_type=MESH)

    @pl.when(z < depth - 1)
    def _():
        pl.semaphore_signal(barrier, inc=1, device_id={"seq": me + 4}, device_id_type=MESH)

    first, second = starts[0, 0], starts[0, 1]
    last = (first < rows).astype(jnp.int32) + (second < rows).astype(jnp.int32)
    take_one = jnp.where(last == 1, 1.0, 0.0)
    take_two = jnp.where(last == 2, 1.0, 0.0)
    here = jnp.where(last > 0, 1.0, 0.0)

    def segments(shape, dim):
        position = lax.broadcasted_iota(jnp.int32, shape, dim)
        one = jnp.where(position >= first, 1, 0)
        return position, one + jnp.where(position >= second, 1, 0)

    row_pos, row_seg = segments((rows, rows), 0)
    col_pos, col_seg = segments((rows, rows), 1)
    allowed[...] = jnp.where((row_pos >= col_pos) & (row_seg == col_seg), 1.0, 0.0)
    _, seg = segments((rows, DIM), 0)
    for i in range(3):
        seg_masks[i] = jnp.where(seg == i, 1.0, 0.0).astype(jnp.bfloat16)
    seg_masks[3] = jnp.where(seg == last, 1.0, 0.0).astype(jnp.bfloat16)
    acc[...] = jnp.zeros_like(acc)
    flags[0] = jnp.full((8, DIM), here, jnp.float32)

    @pl.when(z == 0)
    def _():
        z_in[...] = jnp.zeros_like(z_in)

    neighbours = 2 + jnp.where(z > 0, 1, 0) + jnp.where(z < depth - 1, 1, 0)
    pl.semaphore_wait(barrier, neighbours)

    def remote(kind, slot, source, target, device):
        return pltpu.make_async_remote_copy(
            src_ref=source, dst_ref=target, send_sem=send_sem.at[kind, slot],
            recv_sem=recv_sem.at[kind, slot], device_id={"seq": device}, device_id_type=MESH,
        )

    def flag_copy(slot, source, target, device):
        return pltpu.make_async_remote_copy(
            src_ref=flags.at[source], dst_ref=flags.at[target], send_sem=flag_send.at[slot],
            recv_sem=flag_recv.at[slot], device_id={"seq": device}, device_id_type=MESH,
        )

    def near_a_copy(i):
        return remote(0, i, state.at[part_diag * PART + i], near_a.at[i], partner)

    def near_b_copy(i):
        return remote(1, i, state.at[part_near * PART + i], near_b.at[i], partner)

    def chip_copy(i):
        return remote(2, i, chip_out.at[i], chip_in.at[i], across)

    def z_copy(i):
        return remote(3, i, z_out.at[i], z_in.at[i], following)

    def back_copy(i):
        return remote(4, i, back_out.at[i], back_in.at[i], across)

    def final_a_send(i):
        return remote(5, i, final_a.at[i], incoming.at[mine * PART + i], partner)

    def final_a_recv(i):
        return remote(5, i, final_a.at[i], incoming.at[part_near * PART + i], partner)

    def final_b_send(i):
        return remote(6, i, final_b.at[i], incoming.at[part_far * PART + i], partner)

    def final_b_recv(i):
        return remote(6, i, final_b.at[i], incoming.at[part_diag * PART + i], partner)

    near_flag = flag_copy(0, 0, 1, partner)
    near_flag.start()

    def lanes(head):
        return pl.ds(pl.multiple_of(head * DIM, DIM), DIM)

    def summarise(head):
        at = lanes(head)
        feature = silu(k[:, at])
        k[:, at] = feature
        total = lax.dot_general(
            feature * seg_masks[3], v[:, at], (((0,), (0,)), ((), ())),
            preferred_element_type=jnp.float32,
        )
        state[head] = (
            total + take_one * c[0, head].astype(jnp.float32)
            + take_two * c[1, head].astype(jnp.float32)
        )

    for i in range(2):
        k_loads[i].wait()
        v_loads[i].wait()
        c_loads[i].wait()

    summarise(part_diag * PART)
    near_a_copy(0).start()

    near_flag.wait_recv()
    is_one = jnp.where(core == 1, 1.0, 0.0)
    keep_me = 1.0 - flags[0]
    keep_near = 1.0 - flags[1]
    coefs[0] = jnp.where(core == 1, keep_me, keep_near)
    coefs[1] = jnp.where(core == 1, keep_near, keep_me)
    coefs[2] = keep_me * keep_near
    flags[2] = keep_me * keep_near
    across_flag = flag_copy(1, 2, 3, across)
    across_flag.start()

    def chip_sum(head, near):
        keep = coefs[0, 0:1, :]
        own_scale = jnp.where(core == 1, jnp.ones_like(keep), keep)
        near_scale = jnp.where(core == 1, keep, jnp.ones_like(keep))
        return state[head] * own_scale + near * near_scale

    @pl.loop(0, PART)
    def _(i):
        @pl.when(i < PART - 1)
        def _():
            summarise(part_diag * PART + i + 1)
            near_a_copy(i + 1).start()

        summarise(part_far * PART + i)
        near_a_copy(i).wait_recv()
        chip_out[i] = chip_sum(part_far * PART + i, near_a[i])
        chip_copy(i).start()

    for i in range(2, 4):
        k_loads[i].wait()
        v_loads[i].wait()
        c_loads[i].wait()
    summarise(part_near * PART)
    near_b_copy(0).start()
    across_flag.wait_recv()
    own_keep = coefs[2]
    far_keep = flags[3]
    coefs[3] = jnp.where(y == 0, own_keep, far_keep)
    coefs[4] = jnp.where(y == 0, far_keep, own_keep)
    coefs[5] = own_keep * far_keep

    @pl.loop(0, PART)
    def _(i):
        @pl.when(i < PART - 1)
        def _():
            summarise(part_near * PART + i + 1)
            near_b_copy(i + 1).start()

        summarise(mine * PART + i)
        near_b_copy(i).wait_recv()
        chip_own[i] = chip_sum(mine * PART + i, near_b[i])

    def local(head):
        at = lanes(head)
        feature = silu(q[:, at])
        q[:, at] = feature * seg_masks[0]
        scores = lax.dot_general(
            feature, k[:, at], (((1,), (1,)), ((), ())), preferred_element_type=jnp.float32
        )
        scores = (scores * allowed[...]).astype(jnp.bfloat16)
        resumed = jnp.concatenate([feature * seg_masks[1], feature * seg_masks[2]], axis=1)
        carried = jnp.concatenate([c[0, head], c[1, head]], axis=0)
        o[:, at] = jnp.dot(scores, v[:, at], preferred_element_type=jnp.float32) + jnp.dot(
            resumed, carried, preferred_element_type=jnp.float32
        )

    def cross(head):
        at = lanes(head)
        wide = incoming[head]
        high = wide.astype(jnp.bfloat16)
        low = (wide - high.astype(jnp.float32)).astype(jnp.bfloat16)
        query = q[:, at]
        total = o[:, at] + jnp.dot(
            jnp.concatenate([query, query], axis=1),
            jnp.concatenate([high, low], axis=0),
            preferred_element_type=jnp.float32,
        )
        o[:, at] = total
        acc[...] += total * total

    def pair(chip_state, head, near):
        keep = coefs[1, 0:1, :]
        one = jnp.ones_like(keep)
        zero = jnp.zeros_like(keep)
        at_one = core == 1
        own = chip_state * jnp.where(at_one, keep, one) + near * jnp.where(at_one, one, zero)
        other = chip_state * jnp.where(at_one, one, keep) + state[head] * jnp.where(
            at_one, zero, one
        )
        return own, other

    def row_step(i):
        chip_copy(i).wait_recv()
        keep = coefs[4, 0:1, :]
        one = jnp.ones_like(keep)
        row[i] = chip_own[i] * jnp.where(y == 0, keep, one) + chip_in[i] * jnp.where(
            y == 0, one, keep
        )

    def prefix_step(i):
        @pl.when(z > 0)
        def _():
            z_copy(i).wait_recv()

        before = z_in[i]
        z_out[i] = row[i] + before * coefs[5, 0:1, :]

        @pl.when(z < depth - 1)
        def _():
            z_copy(i).start()

        keep = coefs[3, 0:1, :]
        one = jnp.ones_like(keep)
        zero = jnp.zeros_like(keep)
        at_one = y == 1
        back_out[i] = before * jnp.where(at_one, one, keep) + chip_own[i] * jnp.where(
            at_one, zero, one
        )
        back_copy(i).start()
        chip_state = before * jnp.where(at_one, keep, one) + chip_in[i] * jnp.where(
            at_one, one, zero
        )
        head = mine * PART + i
        own, other = pair(chip_state, head, near_b[i])
        final_a[i] = other
        final_a_send(i).start()
        incoming[head] = own
        cross(head)

    def near_step(i):
        final_a_recv(i).wait_recv()
        cross(part_near * PART + i)

    def back_step(i):
        back_copy(i).wait_recv()
        head = part_far * PART + i
        own, other = pair(back_in[i], head, near_a[i])
        final_b[i] = other
        final_b_send(i).start()
        incoming[head] = own
        cross(head)

    def diag_step(i):
        final_b_recv(i).wait_recv()
        cross(part_diag * PART + i)

    skew = jnp.minimum(2 * z, 6)
    for i in range(4):
        q_loads[i].wait()

    @pl.loop(0, PART + LAG + 1)
    def _(t):
        @pl.when(t < PART)
        def _():
            local(mine * PART + t)
            local(part_near * PART + t)
            row_step(t)

        @pl.when((t >= PART) & (t < 2 * PART))
        def _():
            local(part_far * PART + t - PART)
            local(part_diag * PART + t - PART)

        @pl.when((t >= skew) & (t < skew + PART))
        def _():
            prefix_step(t - skew)

        @pl.when((t >= skew + 1) & (t < skew + 1 + PART))
        def _():
            near_step(t - skew - 1)

        @pl.when((t >= LAG) & (t < LAG + PART))
        def _():
            back_step(t - LAG)

        @pl.when(t >= LAG + 1)
        def _():
            diag_step(t - LAG - 1)

    def out_copy(i):
        span = pl.ds(pl.multiple_of(i * ROWS_OUT, ROWS_OUT), ROWS_OUT)
        return pltpu.make_async_copy(obuf.at[span], out_hbm.at[span], out_sem.at[i])

    @pl.loop(0, rows // ROWS_OUT)
    def _(i):
        span = pl.ds(pl.multiple_of(i * ROWS_OUT, ROWS_OUT), ROWS_OUT)
        square = jnp.sum(acc[span, :], axis=1, keepdims=True) * (1.0 / (HEADS * DIM))
        scale = lax.rsqrt(square + EPSILON)
        obuf[span, :] = (o[span, :] * scale * gain[...]).astype(jnp.bfloat16)
        out_copy(i).start()

    near_flag.wait_send()
    across_flag.wait_send()

    @pl.loop(0, PART)
    def _(i):
        near_a_copy(i).wait_send()
        near_b_copy(i).wait_send()
        chip_copy(i).wait_send()

        @pl.when(z < depth - 1)
        def _():
            z_copy(i).wait_send()

        back_copy(i).wait_send()
        final_a_send(i).wait_send()
        final_b_send(i).wait_send()

    @pl.loop(0, rows // ROWS_OUT)
    def _(i):
        out_copy(i).wait()


def on_device(queries, keys, values, doc_starts, previous_window_states, out_gain):
    rows, width = queries.shape
    bf16, f32 = jnp.bfloat16, jnp.float32
    part = pltpu.VMEM((PART, DIM, DIM), f32)
    everywhere = pl.BlockSpec(memory_space=pl.ANY)
    return pl.pallas_call(
        kernel,
        out_shape=jax.ShapeDtypeStruct((rows, width), bf16),
        in_specs=[pl.BlockSpec(memory_space=pltpu.SMEM)] + [everywhere] * 4
        + [pl.BlockSpec(memory_space=pltpu.VMEM)],
        out_specs=everywhere,
        scratch_shapes=[
            pltpu.VMEM((rows, width), bf16),
            pltpu.VMEM((rows, width), bf16),
            pltpu.VMEM((rows, width), bf16),
            pltpu.VMEM((2, HEADS, DIM, DIM), bf16),
            pltpu.VMEM((rows, width), f32),
            pltpu.VMEM((rows, width), bf16),
            pltpu.VMEM((rows, DIM), f32),
            pltpu.VMEM((rows, rows), f32),
            pltpu.VMEM((4, rows, DIM), bf16),
            pltpu.VMEM((4, 8, DIM), f32),
            pltpu.VMEM((6, 8, DIM), f32),
            pltpu.VMEM((HEADS, DIM, DIM), f32),
        ] + [part] * 12 + [
            pltpu.VMEM((HEADS, DIM, DIM), f32),
            pltpu.SemaphoreType.DMA((16,)),
            pltpu.SemaphoreType.DMA((rows // ROWS_OUT,)),
            pltpu.SemaphoreType.DMA((2,)),
            pltpu.SemaphoreType.DMA((2,)),
            pltpu.SemaphoreType.DMA((7, PART)),
            pltpu.SemaphoreType.DMA((7, PART)),
        ],
        compiler_params=pltpu.CompilerParams(
            collective_id=0, has_side_effects=True, vmem_limit_bytes=56 * 1024 * 1024
        ),
        cost_estimate=pl.CostEstimate(
            flops=4 * 10**9, bytes_accessed=13 * 10**6, transcendentals=3 * 10**6
        ),
    )(doc_starts, queries, keys, values, previous_window_states, out_gain.reshape(1, width))


def solution(mesh):
    placed = (
        P(("groups", "seq"), None),
        P(("groups", "seq"), None),
        P(("groups", "seq"), None),
        P(("groups", "seq"), None),
        P(("groups", "seq"), None, None, None),
        P(),
    )
    return jax.shard_map(
        on_device, mesh=mesh, in_specs=placed, out_specs=P(("groups", "seq"), None), check_vma=False
    )
```

time: 276 us -> 47.1 us (0.17)
  waiting for transfers between devices: 185 us -> 0 us
  starting transfers between devices: 43.4 us -> 0 us
  Pallas kernels: 0 us -> 43.3 us
  matrix products: 29.3 us -> 0 us
  other arithmetic: 12.8 us -> 0 us
  between operations: 4.01 us -> 0.01 us
  local copies, waits for them, and re-layouts: 0.51 us -> 3.53 us
    ppermute x9 -> x0, waiting for transfers between devices: 185 us -> none  [from_behind(): lax.ppermute(value, axis, [(source, source + steps) for source in range(f...]
    ppermute x9 -> x0, starting transfers between devices: 43.4 us -> none  [from_behind(): lax.ppermute(value, axis, [(source, source + steps) for source in range(f...]
    pallas_call x0 -> x1, Pallas kernels: none -> 43.3 us  [on_device(): pl.pallas_call(kernel, out_shape=jax.ShapeDtypeStruct((rows, width), bf16...]
    dot_general x4 -> x0, matrix products: 29.3 us -> none  [the longest x1 12.9 us: on_device(): jnp.einsum('thd,hde->the', query_wide, incoming, precision=lax.Precision....]
    select_n x3 -> x0, other arithmetic: 4.54 us -> none  [combine(): jnp.where(later[0][0] > 0, later[1], earlier[1] + later[1])]
    reduce_sum x3 -> x0, other arithmetic: 4.54 us -> none  [the longest x1 2.36 us: block_terms(): jnp.sum(picked[:, None, None, None] * carried_block.astype(jnp.float32),...]
    unnamed x10 -> x1, local copies, waits for them, and re-layouts: 0.51 us -> 3.53 us
    convert_element_type x2 -> x0, other arithmetic: 2.92 us -> none  [the longest x1 2.14 us: on_device(): (flat * lax.rsqrt(mean_square + EPSILON) * out_gain).astype(jnp.bfloat16)]
  transfers between devices with their start and end apart: 9 -> 0, of which waited for: 6 -> 0; matrix products, arithmetic and copies ran while one was open for 5% -> 0% of each run, Pallas kernels for 0% -> 0%
where the time goes in v1:
time: 47.1 us; the launch traced here: 46.9 us
  Pallas kernels  43.3 us (92%)
  local copies, waits for them, and re-layouts  3.53 us (7%)
    pallas_call x1, Pallas kernels, on_device(): pl.pallas_call(kernel, out_shape=jax.ShapeDtypeStruct((rows, width), bf16...  43.3 us
    unnamed x1, local copies, waits for them, and re-layouts  3.53 us

profile of v1, /device:TPU:27, one launch (start us, length us, event | category | flops | bytes accessed | tf_op | source)
XLA Modules:
  0.0 46.9 jit_solution(13999364929388626260)
XLA Ops:
  0.0 43.3 %shard_map.64 = bf16[320,4096]{1,0:T(8,128)(2,1)} custom-call(s32[1,2]{1,0:T(1,128)} %starts.1, bf16[320,4096]{1,0:T(8,128)(2,1)} %q_hbm.1, bf16[320,4096]{1,0:T(8,128)(2,1)} %k_hbm.1, bf16[320,4096]{1,0:T(8,128)(2,1)} %v_hbm.1, bf16[2,32,128,128]{3,2,1,0:T(8,128)(2,1)} %c_hbm.1, f32[1,4096]{1,0:T(1,128)} %bitcast.1), custom_call_target="tpu_custom_call" | custom-call | flops 4000000000 | bytes 13000000 | tf_op jit(solution)/shard_map/pallas_call | solution.py:392
  43.4 3.5 %copy.8 = bf16[320,4096]{1,0:T(8,128)(2,1)} copy(bf16[320,4096]{1,0:T(8,128)(2,1)} %shard_map.64) | data formatting | bytes 5242880

commit v2 on v1

--- a/solution.py
+++ b/solution.py
@@ -1,5 +1,3 @@
-import functools
-
 import jax
 import jax.numpy as jnp
 from jax import lax
@@ -12,7 +10,6 @@
 PART = HEADS // 4
 EPSILON = 1e-06
 LAG = 9
-ROWS_OUT = 32
 MESH = pl.DeviceIdType.MESH
 
 
@@ -22,8 +19,8 @@
 
 
 def kernel(
-    starts, q_hbm, k_hbm, v_hbm, c_hbm, gain, out_hbm,
-    q, k, v, c, o, obuf, acc, allowed, seg_masks, flags, coefs,
+    starts, q_hbm, k_hbm, v_hbm, c_hbm, out_hbm, acc,
+    q, k, v, c, o, obuf, allowed, seg_masks, flags, coefs,
     state, near_a, near_b, chip_out, chip_own, chip_in, row, z_in, z_out, back_out, back_in,
     final_a, final_b, incoming,
     in_sem, out_sem, flag_send, flag_recv, send_sem, recv_sem,
@@ -237,6 +234,10 @@
             resumed, carried, preferred_element_type=jnp.float32
         )
 
+    def out_copy(head):
+        at = lanes(head)
+        return pltpu.make_async_copy(obuf.at[:, at], out_hbm.at[:, at], out_sem.at[head])
+
     def cross(head):
         at = lanes(head)
         wide = incoming[head]
@@ -248,8 +249,9 @@
             jnp.concatenate([high, low], axis=0),
             preferred_element_type=jnp.float32,
         )
-        o[:, at] = total
         acc[...] += total * total
+        obuf[:, at] = total.astype(jnp.bfloat16)
+        out_copy(head).start()
 
     def pair(chip_state, head, near):
         keep = coefs[1, 0:1, :]
@@ -350,18 +352,6 @@
         def _():
             diag_step(t - LAG - 1)
 
-    def out_copy(i):
-        span = pl.ds(pl.multiple_of(i * ROWS_OUT, ROWS_OUT), ROWS_OUT)
-        return pltpu.make_async_copy(obuf.at[span], out_hbm.at[span], out_sem.at[i])
-
-    @pl.loop(0, rows // ROWS_OUT)
-    def _(i):
-        span = pl.ds(pl.multiple_of(i * ROWS_OUT, ROWS_OUT), ROWS_OUT)
-        square = jnp.sum(acc[span, :], axis=1, keepdims=True) * (1.0 / (HEADS * DIM))
-        scale = lax.rsqrt(square + EPSILON)
-        obuf[span, :] = (o[span, :] * scale * gain[...]).astype(jnp.bfloat16)
-        out_copy(i).start()
-
     near_flag.wait_send()
     across_flag.wait_send()
 
@@ -379,7 +369,7 @@
         final_a_send(i).wait_send()
         final_b_send(i).wait_send()
 
-    @pl.loop(0, rows // ROWS_OUT)
+    @pl.loop(0, HEADS)
     def _(i):
         out_copy(i).wait()
 
@@ -389,12 +379,14 @@
     bf16, f32 = jnp.bfloat16, jnp.float32
     part = pltpu.VMEM((PART, DIM, DIM), f32)
     everywhere = pl.BlockSpec(memory_space=pl.ANY)
-    return pl.pallas_call(
+    total, square = pl.pallas_call(
         kernel,
-        out_shape=jax.ShapeDtypeStruct((rows, width), bf16),
-        in_specs=[pl.BlockSpec(memory_space=pltpu.SMEM)] + [everywhere] * 4
-        + [pl.BlockSpec(memory_space=pltpu.VMEM)],
-        out_specs=everywhere,
+        out_shape=(
+            jax.ShapeDtypeStruct((rows, width), bf16),
+            jax.ShapeDtypeStruct((rows, DIM), f32),
+        ),
+        in_specs=[pl.BlockSpec(memory_space=pltpu.SMEM)] + [everywhere] * 4,
+        out_specs=(everywhere, pl.BlockSpec(memory_space=pltpu.VMEM)),
         scratch_shapes=[
             pltpu.VMEM((rows, width), bf16),
             pltpu.VMEM((rows, width), bf16),
@@ -402,7 +394,6 @@
             pltpu.VMEM((2, HEADS, DIM, DIM), bf16),
             pltpu.VMEM((rows, width), f32),
             pltpu.VMEM((rows, width), bf16),
-            pltpu.VMEM((rows, DIM), f32),
             pltpu.VMEM((rows, rows), f32),
             pltpu.VMEM((4, rows, DIM), bf16),
             pltpu.VMEM((4, 8, DIM), f32),
@@ -411,7 +402,7 @@
         ] + [part] * 12 + [
             pltpu.VMEM((HEADS, DIM, DIM), f32),
             pltpu.SemaphoreType.DMA((16,)),
-            pltpu.SemaphoreType.DMA((rows // ROWS_OUT,)),
+            pltpu.SemaphoreType.DMA((HEADS,)),
             pltpu.SemaphoreType.DMA((2,)),
             pltpu.SemaphoreType.DMA((2,)),
             pltpu.SemaphoreType.DMA((7, PART)),
@@ -423,7 +414,9 @@
         cost_estimate=pl.CostEstimate(
             flops=4 * 10**9, bytes_accessed=13 * 10**6, transcendentals=3 * 10**6
         ),
-    )(doc_starts, queries, keys, values, previous_window_states, out_gain.reshape(1, width))
+    )(doc_starts, queries, keys, values, previous_window_states)
+    mean_square = jnp.sum(square, axis=1, keepdims=True) / width
+    return (total.astype(f32) * lax.rsqrt(mean_square + EPSILON) * out_gain).astype(bf16)
 
 
 def solution(mesh):

time: 47.1 us -> 48 us (1.019)
  other arithmetic: 0 us -> 5.17 us
  local copies, waits for them, and re-layouts: 3.53 us -> 0.01 us
  Pallas kernels: 43.3 us -> 42.6 us
    convert_element_type x0 -> x1, other arithmetic: none -> 4.1 us  [on_device(): (total.astype(f32) * lax.rsqrt(mean_square + EPSILON) * out_gain).astype(...]
    unnamed x1 -> x2, local copies, waits for them, and re-layouts: 3.53 us -> 0.01 us
    reduce_sum x0 -> x1, other arithmetic: none -> 1.06 us  [on_device(): mean_square = jnp.sum(square, axis=1, keepdims=True) / width]
    pallas_call x1, Pallas kernels: 43.3 us -> 42.6 us  [on_device(): pl.pallas_call(kernel, out_shape=(jax.ShapeDtypeStruct((rows, width), bf1...]
where the time goes in v2:
time: 48 us; the launch traced here: 47.8 us
  Pallas kernels  42.6 us (89%)
  other arithmetic  5.17 us (11%)
    pallas_call x1, Pallas kernels, on_device(): pl.pallas_call(kernel, out_shape=(jax.ShapeDtypeStruct((rows, width), bf1...  42.6 us
    convert_element_type x1, other arithmetic, on_device(): (total.astype(f32) * lax.rsqrt(mean_square + EPSILON) * out_gain).astype(...  4.1 us
    reduce_sum x1, other arithmetic, on_device(): mean_square = jnp.sum(square, axis=1, keepdims=True) / width  1.06 us

profile of v2, /device:TPU:27, one launch (start us, length us, event | category | flops | bytes accessed | tf_op | source)
XLA Modules:
  0.0 47.8 jit_solution(1081634935946359037)
XLA Ops:
  0.0 0.0 copy-start
  0.0 42.6 %shard_map.64 = (bf16[320,4096]{1,0:T(8,128)(2,1)}, f32[320,128]{1,0:T(8,128)}) custom-call(s32[1,2]{1,0:T(1,128)} %starts.1, bf16[320,4096]{1,0:T(8,128)(2,1)} %q_hbm.1, bf16[320,4096]{1,0:T(8,128)(2,1)} %k_hbm.1, bf16[320,4096]{1,0:T(8,128)(2,1)} %v_hbm.1, bf16[2,32,128,128]{3,2,1,0:T(8,128)(2,1)} %c_hbm.1), custom_call_target="tpu_custom_call" | custom-call | flops 4000000000 | bytes 13000000 | tf_op jit(solution)/shard_map/pallas_call | solution.py:382
  42.6 1.1 %reduce_sum.9 = f32[320]{0:T(512)S(1)} reduce(f32[320,128]{1,0:T(8,128)} %get-tuple-element.8, f32[]{:T(128)} %constant.1.clone.1), dimensions={1}, to_apply=%region_0.0 | reduce | flops 40640 | bytes 165124 | tf_op jit(solution)/shard_map/reduce_sum | solution.py:418
  43.7 0.0 copy-done
  43.7 4.1 %multiply_convert_fusion = bf16[320,4096]{1,0:T(8,128)(2,1)} fusion(bf16[320,4096]{1,0:T(8,128)(2,1)} %get-tuple-element.7, f32[4096]{0:T(1024)S(1)} %copy-done, f32[320]{0:T(512)S(1)} %add_rsqrt_fusion), kind=kLoop, calls=%fused_computation | loop fusion | flops 5242880 | bytes 5260544 | tf_op jit(solution)/shard_map/convert_element_type | solution.py:419
  (1 shorter events, 0.0 us)
Async XLA Ops:
  0.0 43.7 %copy-start = (f32[4096]{0:T(1024)S(1)}, f32[4096]{0:T(1024)}, u32[]{:S(2)}) copy-start(f32[4096]{0:T(1024)} %param.11) | copy-start | bytes 49156

commit v3 on v1

--- a/solution.py
+++ b/solution.py
@@ -1,5 +1,3 @@
-import functools
-
 import jax
 import jax.numpy as jnp
 from jax import lax
@@ -149,26 +147,31 @@
     def lanes(head):
         return pl.ds(pl.multiple_of(head * DIM, DIM), DIM)
 
-    def summarise(head):
-        at = lanes(head)
-        feature = silu(k[:, at])
-        k[:, at] = feature
-        total = lax.dot_general(
-            feature * seg_masks[3], v[:, at], (((0,), (0,)), ((), ())),
-            preferred_element_type=jnp.float32,
-        )
-        state[head] = (
-            total + take_one * c[0, head].astype(jnp.float32)
+    def summarise(*heads):
+        features = [silu(k[:, lanes(head)]) for head in heads]
+        tails = [feature * seg_masks[3] for feature in features]
+        totals = [
+            lax.dot_general(
+                tail, v[:, lanes(head)], (((0,), (0,)), ((), ())),
+                preferred_element_type=jnp.float32,
+            )
+            + take_one * c[0, head].astype(jnp.float32)
             + take_two * c[1, head].astype(jnp.float32)
-        )
-
-    for i in range(2):
+            for tail, head in zip(tails, heads)
+        ]
+        for head, feature, total in zip(heads, features, totals):
+            k[:, lanes(head)] = feature
+            state[head] = total
+
+    def arrive(i):
         k_loads[i].wait()
         v_loads[i].wait()
         c_loads[i].wait()
 
+    arrive(0)
     summarise(part_diag * PART)
     near_a_copy(0).start()
+    arrive(1)
 
     near_flag.wait_recv()
     is_one = jnp.where(core == 1, 1.0, 0.0)
@@ -187,22 +190,22 @@
         near_scale = jnp.where(core == 1, keep, jnp.ones_like(keep))
         return state[head] * own_scale + near * near_scale
 
-    @pl.loop(0, PART)
-    def _(i):
-        @pl.when(i < PART - 1)
-        def _():
-            summarise(part_diag * PART + i + 1)
-            near_a_copy(i + 1).start()
-
-        summarise(part_far * PART + i)
+    def chip_step(i):
         near_a_copy(i).wait_recv()
         chip_out[i] = chip_sum(part_far * PART + i, near_a[i])
         chip_copy(i).start()
 
-    for i in range(2, 4):
-        k_loads[i].wait()
-        v_loads[i].wait()
-        c_loads[i].wait()
+    @pl.loop(0, PART - 1)
+    def _(i):
+        summarise(part_diag * PART + i + 1, part_far * PART + i)
+        near_a_copy(i + 1).start()
+        chip_step(i)
+
+    summarise(part_far * PART + PART - 1)
+    chip_step(PART - 1)
+
+    arrive(2)
+    arrive(3)
     summarise(part_near * PART)
     near_b_copy(0).start()
     across_flag.wait_recv()
@@ -212,44 +215,68 @@
     coefs[4] = jnp.where(y == 0, far_keep, own_keep)
     coefs[5] = own_keep * far_keep
 
-    @pl.loop(0, PART)
-    def _(i):
-        @pl.when(i < PART - 1)
-        def _():
-            summarise(part_near * PART + i + 1)
-            near_b_copy(i + 1).start()
-
-        summarise(mine * PART + i)
+    def own_step(i):
         near_b_copy(i).wait_recv()
         chip_own[i] = chip_sum(mine * PART + i, near_b[i])
 
-    def local(head):
-        at = lanes(head)
-        feature = silu(q[:, at])
-        q[:, at] = feature * seg_masks[0]
-        scores = lax.dot_general(
-            feature, k[:, at], (((1,), (1,)), ((), ())), preferred_element_type=jnp.float32
-        )
-        scores = (scores * allowed[...]).astype(jnp.bfloat16)
-        resumed = jnp.concatenate([feature * seg_masks[1], feature * seg_masks[2]], axis=1)
-        carried = jnp.concatenate([c[0, head], c[1, head]], axis=0)
-        o[:, at] = jnp.dot(scores, v[:, at], preferred_element_type=jnp.float32) + jnp.dot(
-            resumed, carried, preferred_element_type=jnp.float32
-        )
-
-    def cross(head):
-        at = lanes(head)
-        wide = incoming[head]
-        high = wide.astype(jnp.bfloat16)
-        low = (wide - high.astype(jnp.float32)).astype(jnp.bfloat16)
-        query = q[:, at]
-        total = o[:, at] + jnp.dot(
-            jnp.concatenate([query, query], axis=1),
-            jnp.concatenate([high, low], axis=0),
-            preferred_element_type=jnp.float32,
-        )
-        o[:, at] = total
-        acc[...] += total * total
+    @pl.loop(0, PART - 1)
+    def _(i):
+        summarise(part_near * PART + i + 1, mine * PART + i)
+        near_b_copy(i + 1).start()
+        own_step(i)
+
+    summarise(mine * PART + PART - 1)
+    own_step(PART - 1)
+
+    def local(*heads):
+        features = [silu(q[:, lanes(head)]) for head in heads]
+        scores = [
+            lax.dot_general(
+                feature, k[:, lanes(head)], (((1,), (1,)), ((), ())),
+                preferred_element_type=jnp.float32,
+            )
+            for feature, head in zip(features, heads)
+        ]
+        resumed = [
+            jnp.dot(
+                jnp.concatenate([feature * seg_masks[1], feature * seg_masks[2]], axis=1),
+                jnp.concatenate([c[0, head], c[1, head]], axis=0),
+                preferred_element_type=jnp.float32,
+            )
+            for feature, head in zip(features, heads)
+        ]
+        permitted = allowed[...]
+        scores = [(score * permitted).astype(jnp.bfloat16) for score in scores]
+        totals = [
+            jnp.dot(score, v[:, lanes(head)], preferred_element_type=jnp.float32) + term
+            for score, head, term in zip(scores, heads, resumed)
+        ]
+        first_only = [feature * seg_masks[0] for feature in features]
+        for head, feature, total in zip(heads, first_only, totals):
+            q[:, lanes(head)] = feature
+            o[:, lanes(head)] = total
+
+    def cross(*heads):
+        totals = []
+        for head in heads:
+            wide = incoming[head]
+            high = wide.astype(jnp.bfloat16)
+            low = (wide - high.astype(jnp.float32)).astype(jnp.bfloat16)
+            query = q[:, lanes(head)]
+            totals.append(
+                o[:, lanes(head)]
+                + jnp.dot(
+                    jnp.concatenate([query, query], axis=1),
+                    jnp.concatenate([high, low], axis=0),
+                    preferred_element_type=jnp.float32,
+                )
+            )
+        squares = acc[...]
+        for total in totals:
+            squares = squares + total * total
+        acc[...] = squares
+        for head, total in zip(heads, totals):
+            o[:, lanes(head)] = total
 
     def pair(chip_state, head, near):
         keep = coefs[1, 0:1, :]
@@ -298,11 +325,10 @@
         final_a[i] = other
         final_a_send(i).start()
         incoming[head] = own
-        cross(head)
 
     def near_step(i):
         final_a_recv(i).wait_recv()
-        cross(part_near * PART + i)
+        cross(mine * PART + i, part_near * PART + i)
 
     def back_step(i):
         back_copy(i).wait_recv()
@@ -311,11 +337,10 @@
         final_b[i] = other
         final_b_send(i).start()
         incoming[head] = own
-        cross(head)
 
     def diag_step(i):
         final_b_recv(i).wait_recv()
-        cross(part_diag * PART + i)
+        cross(part_far * PART + i, part_diag * PART + i)
 
     skew = jnp.minimum(2 * z, 6)
     for i in range(4):
@@ -325,14 +350,12 @@
     def _(t):
         @pl.when(t < PART)
         def _():
-            local(mine * PART + t)
-            local(part_near * PART + t)
+            local(mine * PART + t, part_near * PART + t)
             row_step(t)
 
         @pl.when((t >= PART) & (t < 2 * PART))
         def _():
-            local(part_far * PART + t - PART)
-            local(part_diag * PART + t - PART)
+            local(part_far * PART + t - PART, part_diag * PART + t - PART)
 
         @pl.when((t >= skew) & (t < skew + PART))
         def _():

time: 47.1 us -> 46.3 us (0.983)
  Pallas kernels: 43.3 us -> 42.5 us
    pallas_call x1, Pallas kernels: 43.3 us -> 42.5 us  [on_device(): pl.pallas_call(kernel, out_shape=jax.ShapeDtypeStruct((rows, width), bf16...]
where the time goes in v3:
time: 46.3 us; the launch traced here: 46 us
  Pallas kernels  42.5 us (92%)
  local copies, waits for them, and re-layouts  3.53 us (8%)
    pallas_call x1, Pallas kernels, on_device(): pl.pallas_call(kernel, out_shape=jax.ShapeDtypeStruct((rows, width), bf16...  42.5 us
    unnamed x1, local copies, waits for them, and re-layouts  3.53 us

profile of v3, /device:TPU:27, one launch (start us, length us, event | category | flops | bytes accessed | tf_op | source)
XLA Modules:
  0.0 46.0 jit_solution(4087375519852078317)
XLA Ops:
  0.0 42.5 %shard_map.64 = bf16[320,4096]{1,0:T(8,128)(2,1)} custom-call(s32[1,2]{1,0:T(1,128)} %starts.1, bf16[320,4096]{1,0:T(8,128)(2,1)} %q_hbm.1, bf16[320,4096]{1,0:T(8,128)(2,1)} %k_hbm.1, bf16[320,4096]{1,0:T(8,128)(2,1)} %v_hbm.1, bf16[2,32,128,128]{3,2,1,0:T(8,128)(2,1)} %c_hbm.1, f32[1,4096]{1,0:T(1,128)} %bitcast.1), custom_call_target="tpu_custom_call" | custom-call | flops 4000000000 | bytes 13000000 | tf_op jit(solution)/shard_map/pallas_call | solution.py:415
  42.5 3.5 %copy.8 = bf16[320,4096]{1,0:T(8,128)(2,1)} copy(bf16[320,4096]{1,0:T(8,128)(2,1)} %shard_map.64) | data formatting | bytes 5242880

commit v4 on v3

--- a/solution.py
+++ b/solution.py
@@ -350,24 +350,27 @@
     def _(t):
         @pl.when(t < PART)
         def _():
+            row_step(t)
+
+        @pl.when((t >= skew) & (t < skew + PART))
+        def _():
+            prefix_step(t - skew)
+
+        @pl.when((t >= LAG) & (t < LAG + PART))
+        def _():
+            back_step(t - LAG)
+
+        @pl.when(t < PART)
+        def _():
             local(mine * PART + t, part_near * PART + t)
-            row_step(t)
 
         @pl.when((t >= PART) & (t < 2 * PART))
         def _():
             local(part_far * PART + t - PART, part_diag * PART + t - PART)
 
-        @pl.when((t >= skew) & (t < skew + PART))
-        def _():
-            prefix_step(t - skew)
-
         @pl.when((t >= skew + 1) & (t < skew + 1 + PART))
         def _():
             near_step(t - skew - 1)
-
-        @pl.when((t >= LAG) & (t < LAG + PART))
-        def _():
-            back_step(t - LAG)
 
         @pl.when(t >= LAG + 1)
         def _():

time: 46.3 us -> 45.8 us (0.989)
  no operation moved by 1% of the time
where the time goes in v4:
time: 45.8 us; the launch traced here: 45.6 us
  Pallas kernels  42.1 us (92%)
  local copies, waits for them, and re-layouts  3.53 us (8%)
    pallas_call x1, Pallas kernels, on_device(): pl.pallas_call(kernel, out_shape=jax.ShapeDtypeStruct((rows, width), bf16...  42.1 us
    unnamed x1, local copies, waits for them, and re-layouts  3.53 us

profile of v4, /device:TPU:27, one launch (start us, length us, event | category | flops | bytes accessed | tf_op | source)
XLA Modules:
  0.0 45.6 jit_solution(9984061581361981985)
XLA Ops:
  0.0 42.1 %shard_map.64 = bf16[320,4096]{1,0:T(8,128)(2,1)} custom-call(s32[1,2]{1,0:T(1,128)} %starts.1, bf16[320,4096]{1,0:T(8,128)(2,1)} %q_hbm.1, bf16[320,4096]{1,0:T(8,128)(2,1)} %k_hbm.1, bf16[320,4096]{1,0:T(8,128)(2,1)} %v_hbm.1, bf16[2,32,128,128]{3,2,1,0:T(8,128)(2,1)} %c_hbm.1, f32[1,4096]{1,0:T(1,128)} %bitcast.1), custom_call_target="tpu_custom_call" | custom-call | flops 4000000000 | bytes 13000000 | tf_op jit(solution)/shard_map/pallas_call | solution.py:418
  42.1 3.5 %copy.8 = bf16[320,4096]{1,0:T(8,128)(2,1)} copy(bf16[320,4096]{1,0:T(8,128)(2,1)} %shard_map.64) | data formatting | bytes 5242880
